TPU v7x, 512 devices: a whole 4x4x16 slice. The times are simulated.
512 devices in a mesh: vis: 16 (over z_lo, core), tp: 8 (over z_hi, x), dp: 4 (over y).
Axes of the slice: x: 4, y: 4, z: 16 (z_hi: 2, z_lo: 8; z = z_hi * 8 + z_lo), core: 2. Of those that a mesh axis runs over, the one named last changes fastest.
Arguments:
- features: bfloat16 [6144, 4, 1280], P('vis', 'dp'), may hold values from -6 to 6
- merge_weight: bfloat16 [4, 1280, 8192], P('dp', None, 'tp'), may hold values from -0.078125 to 0.078125
- gain: float32 [8192], P('tp'), may hold values from 0.1 to 1.9
- positions: int32 [6144], replicated, may hold values from 0 to 8191, as said below
- cotangent: bfloat16 [8192, 8192], P(('vis', 'dp'), 'tp'), may hold values from -6 to 6
Outputs:
- feature_grad: bfloat16 [6144, 4, 1280], P('vis', 'dp')
- weight_grad: bfloat16 [4, 1280, 8192], P('dp', 'vis', 'tp')
Inputs may be any that keep to these rules, and one draw needn't show every extreme that they name: Positions are distinct. Split the rows into aligned blocks of 96 and the positions into owners' ranges of 128: each block sends exactly 2 rows to one owner and spreads the rest as evenly as possible over the other owners, in an order drawn at random.
All inputs are finite; a program needn't handle non-finite values.
Results may differ from a plain program's by a relative error of at most 0.023.
Values may be sent and summed in bfloat16 or wider, within the bound.
A program may use at most 64 MiB of HBM per device.

v0:
```python
import jax
import jax.numpy as jnp
from jax import lax
from jax.sharding import PartitionSpec as P

D = 8192


eps = 1e-06


def routing(positions, slots_dev, per_block, owners):
    total = positions.shape[0]
    owner_of = positions // slots_dev
    onehot = (owner_of[:, None] == jnp.arange(owners, dtype=jnp.int32)[None, :]).astype(jnp.int32)
    counted = jnp.cumsum(onehot.reshape(owners, per_block, owners), axis=1).reshape(total, owners)
    rank_in = jnp.sum(counted * onehot, axis=1) - 1
    source_of = jnp.arange(total, dtype=jnp.int32) // per_block
    return (owner_of, rank_in, source_of)


def norm_backward(rows, cot_rows, gain_full):
    values = rows.astype(jnp.float32)
    scaled = cot_rows.astype(jnp.float32) * gain_full[None, :]
    sq_sum, dot_sum = lax.psum(
        (jnp.sum(values * values, axis=1), jnp.sum(scaled * values, axis=1)), "tp"
    )
    inverse = lax.rsqrt(sq_sum / D + eps)
    grad = inverse[:, None] * scaled - (inverse**3 * dot_sum / D)[:, None] * values
    return grad.astype(jnp.bfloat16)


def on_device(features, merge_weight, gain, positions, cotangent):
    rows_here, sub_count, vis_width = features.shape
    cols_here = merge_weight.shape[2]
    slots_dev = cotangent.shape[0]
    dp_size = lax.axis_size("dp")
    owners = lax.axis_size("vis") * dp_size
    per_block = rows_here // dp_size
    capacity = max(2, (per_block + owners - 1) // owners)
    owner_index = lax.axis_index(("vis", "dp"))
    flat_width = sub_count * vis_width
    flat_x = features.reshape(rows_here, flat_width)
    flat_w = merge_weight.reshape(flat_width, cols_here)
    x_rows = flat_x
    vis_rows = lax.psum_scatter(
        jnp.dot(x_rows, flat_w, preferred_element_type=jnp.float32).astype(jnp.bfloat16),
        "dp",
        scatter_dimension=0,
        tiled=True,
    )
    owner_of, rank_in, source_of = routing(positions, slots_dev, per_block, owners)
    slot_count = owners * capacity
    my_owner = lax.dynamic_slice_in_dim(owner_of, owner_index * per_block, per_block)
    my_rank = lax.dynamic_slice_in_dim(rank_in, owner_index * per_block, per_block)
    send_slot = my_owner * capacity + my_rank
    row_of_slot = (
        jnp.full((slot_count,), per_block, jnp.int32)
        .at[send_slot]
        .set(jnp.arange(per_block, dtype=jnp.int32))
    )
    arriving = owner_of == owner_index
    target = jnp.where(arriving, source_of * capacity + rank_in, slot_count)
    local_pos = positions - owner_index * slots_dev
    pos_of_slot = (
        jnp.full((slot_count,), slots_dev, jnp.int32).at[target].set(local_pos, mode="drop")
    )
    padded_cot = jnp.concatenate([cotangent, jnp.zeros((1, cols_here), cotangent.dtype)], axis=0)
    cot_slots = padded_cot[pos_of_slot]
    padded_rows = jnp.concatenate([vis_rows, jnp.zeros((1, cols_here), jnp.bfloat16)], axis=0)
    arrived = lax.all_to_all(
        padded_rows[row_of_slot], ("vis", "dp"), split_axis=0, concat_axis=0, tiled=True
    )
    grad_slots = norm_backward(arrived, cot_slots, gain)
    returned = lax.all_to_all(grad_slots, ("vis", "dp"), split_axis=0, concat_axis=0, tiled=True)
    grad_rows = returned[send_slot]
    block_rows = lax.all_gather(grad_rows, "dp", axis=0, tiled=True)
    x_rows = flat_x
    weight_acc = lax.dot_general(
        x_rows, block_rows, (((0,), (0,)), ((), ())), preferred_element_type=jnp.float32
    )
    row_part = lax.dot_general(
        block_rows, flat_w, (((1,), (1,)), ((), ())), preferred_element_type=jnp.float32
    )
    feature_grad = lax.psum(row_part.astype(jnp.bfloat16), "tp").reshape(
        rows_here, sub_count, vis_width
    )
    weight_grad = lax.psum_scatter(
        weight_acc.reshape(sub_count, vis_width, cols_here).astype(jnp.bfloat16),
        "vis",
        scatter_dimension=1,
        tiled=True,
    )
    return (feature_grad, weight_grad)


def solution(mesh):
    return jax.shard_map(
        on_device,
        mesh=mesh,
        in_specs=(P("vis", "dp", None), P("dp", None, "tp"), P("tp"), P(), P(("vis", "dp"), "tp")),
        out_specs=(P("vis", "dp", None), P("dp", "vis", "tp")),
        check_vma=False,
    )
```

profile of v0, /device:TPU:6, one launch (start us, length us, event | category | flops | bytes accessed | tf_op | source)
XLA Modules:
  0.0 480.3 jit_solution(6718403317048487212)
XLA Ops:
  7.2 1.7 copy-done
  8.9 3.3 fusion.10
  12.4 3.3 select_reduce_fusion
  16.0 0.9 scatter_custom_fusion
  16.9 30.0 %reduce-scatter.5.cloned.1.call-done = bf16[96,1024]{1,0:T(8,128)(2,1)} async-done(((bf16[384,1024]{1,0:T(8,128)(2,1)}), bf16[96,1024]{1,0:T(8,128)(2,1)}) %reduce-scatter.5.cloned.1.call-update) | async-done | bytes 196624 | tf_op jit(solution)/shard_map/reduce_scatter | solution.py:46
  46.9 0.9 concatenate.6
  47.8 0.9 gather_fusion
  48.7 0.8 all_to_all.12
  49.5 11.9 %all-to-all-start = ((bf16[64,2,1024]{2,1,0:T(2,128)(2,1)}), bf16[64,2,1024]{2,1,0:T(2,128)(2,1)S(1)}, u32[]{:S(2)}, u32[]{:S(2)}) async-start(bf16[64,2,1024]{2,1,0:T(2,128)(2,1)} %all_to_all.12), calls=%async_computation.1 | async-start | bytes 524288 | tf_op jit(solution)/shard_map/all_to_all | solution.py:71
  61.5 23.0 %scatter_custom_fusion.1 = s32[128]{0:T(128)S(1)} fusion(s32[6144]{0:T(1024)S(1)} %get-tuple-element.17, s32[6144]{0:T(1024)S(1)} %get-tuple-element.16, s32[]{:T(128)} %constant.62.clone.1), kind=kCustom, calls=%fused_computation.59 | custom fusion | bytes 516 | tf_op jit(solution)/shard_map/scatter | solution.py:66
  84.5 1.6 gather_fusion.1
  86.0 1.3 reshape.71
  87.3 0.6 fusion.15
  88.0 0.1 reduce_sum.33
  88.1 0.1 reduce_sum.35
  88.2 33.1 %all-reduce.2 = (f32[128]{0:T(128)S(1)}, f32[128]{0:T(128)S(1)}) all-reduce(f32[128]{0:T(128)S(1)} %reduce_sum.35, f32[128]{0:T(128)S(1)} %reduce_sum.33), channel_id=1, replica_groups=mesh['vis'=16,'tp'=8,'dp'=4] {'tp'}, use_global_device_ids=true, to_apply=%region_8.9 | all-reduce | flops 256 | bytes 2048 | tf_op jit(solution)/shard_map/psum | solution.py:25
  121.4 0.1 mul.74
  121.5 0.1 mul.84
  121.7 1.2 fusion.18
  122.8 13.1 %all-to-all-start.1 = ((bf16[64,2,1024]{2,1,0:T(2,128)(2,1)}), bf16[64,2,1024]{2,1,0:T(2,128)(2,1)S(1)}, u32[]{:S(2)}, u32[]{:S(2)}) async-start(bf16[64,2,1024]{2,1,0:T(2,128)(2,1)} %fusion.18), calls=%async_computation.2 | async-start | bytes 524288 | tf_op jit(solution)/shard_map/all_to_all | solution.py:75
  136.1 19.3 %all-to-all-done.1 = bf16[64,2,1024]{2,1,0:T(2,128)(2,1)S(1)} async-done(((bf16[64,2,1024]{2,1,0:T(2,128)(2,1)}), bf16[64,2,1024]{2,1,0:T(2,128)(2,1)S(1)}, u32[]{:S(2)}, u32[]{:S(2)}) %all-to-all-start.1) | async-done | bytes 262176 | tf_op jit(solution)/shard_map/all_to_all | solution.py:75
  155.4 1.5 gather_fusion.2
  156.9 13.9 %all-gather = bf16[384,1024]{1,0:T(8,128)(2,1)S(1)} all-gather(bf16[96,1024]{1,0:T(8,128)(2,1)} %gather_fusion.2), channel_id=2, replica_groups=mesh['vis'=16,'tp'=8,'dp'=4] {'dp'}, dimensions={0}, use_global_device_ids=true | all-gather | bytes 983040 | tf_op jit(solution)/shard_map/all_gather | solution.py:77
  170.8 4.3 fusion
  175.1 11.6 %copy.18 = bf16[1,1280,1024]{2,0,1:T(2,128)(2,1)} copy(bf16[1,1280,1024]{1,2,0:T(8,128)(2,1)} %fusion) | data formatting | bytes 5242880
  186.7 5.0 %copy.23 = bf16[1280,1,1024]{2,0,1:T(8,128)(2,1)} copy(bf16[1280,1,1024]{2,1,0:T(2,128)(2,1)} %bitcast.29) | data formatting | bytes 5242880
  191.8 2.2 fusion.6
  193.9 108.3 %reduce-scatter.7.cloned.1.call-done = bf16[80,1024]{1,0:T(8,128)(2,1)} async-done(((bf16[1280,1024]{1,0:T(8,128)(2,1)}), bf16[80,1024]{1,0:T(8,128)(2,1)}) %reduce-scatter.7.cloned.1.call-update) | async-done | bytes 163856
  302.2 1.1 reshape_bitcast_fusion
  303.3 0.7 copy.17
  304.0 167.6 %all-reduce.5.cloned.1.call-done = bf16[384,1,1280]{2,0,1:T(8,128)(2,1)} async-done(((bf16[384,1,1280]{2,0,1:T(8,128)(2,1)}), bf16[384,1,1280]{2,0,1:T(8,128)(2,1)}) %all-reduce.5.cloned.1.call-update) | async-done | bytes 983056 | tf_op jit(solution)/shard_map/psum | solution.py:85
  471.6 2.2 copy.25
  (31 shorter events, 0.8 us)
Async XLA Ops:
  7.2 1.7 copy-start
  7.2 5.0 %copy-start.2 = (s32[6144]{0:T(1024)S(1)}, s32[6144]{0:T(1024)}, u32[]{:S(2)}) copy-start(s32[6144]{0:T(1024)} %param.8) | copy-start | bytes 73732
  7.2 39.7 %reduce-scatter.5.cloned.1.call-start = ((), (), s32[]{:S(2)}) async-start(), calls=%async_computation.4 | async-start | bytes 983040 | tf_op jit(solution)/shard_map/reduce_scatter | solution.py:46
  12.2 49.2 %copy-start.1 = (bf16[128,1024]{1,0:T(8,128)(2,1)S(1)}, bf16[128,1024]{1,0:T(8,128)(2,1)}, u32[]{:S(2)}) copy-start(bf16[128,1024]{1,0:T(8,128)(2,1)} %param.9) | copy-start | bytes 786436
  48.7 38.6 %copy-start.3 = (f32[1024]{0:T(1024)S(1)}, f32[1024]{0:T(1024)}, u32[]{:S(2)}) copy-start(f32[1024]{0:T(1024)} %param.7) | copy-start | bytes 12292
  49.5 37.8 %all-to-all-start = ((bf16[64,2,1024]{2,1,0:T(2,128)(2,1)}), bf16[64,2,1024]{2,1,0:T(2,128)(2,1)S(1)}, u32[]{:S(2)}, u32[]{:S(2)}) async-start(bf16[64,2,1024]{2,1,0:T(2,128)(2,1)} %all_to_all.12), calls=%async_computation.1 | async-start | bytes 524288 | tf_op jit(solution)/shard_map/all_to_all | solution.py:71
  122.8 32.5 %all-to-all-start.1 = ((bf16[64,2,1024]{2,1,0:T(2,128)(2,1)}), bf16[64,2,1024]{2,1,0:T(2,128)(2,1)S(1)}, u32[]{:S(2)}, u32[]{:S(2)}) async-start(bf16[64,2,1024]{2,1,0:T(2,128)(2,1)} %fusion.18), calls=%async_computation.2 | async-start | bytes 524288 | tf_op jit(solution)/shard_map/all_to_all | solution.py:75
  136.0 166.2 %reduce-scatter.7.cloned.1.call-start = ((), (), s32[]{:S(2)}) async-start(), calls=%async_computation.6 | async-start | bytes 2785280
  191.7 279.9 %all-reduce.5.cloned.1.call-start = ((), (), s32[]{:S(2)}) async-start(), calls=%async_computation.5 | async-start | bytes 1966080 | tf_op jit(solution)/shard_map/psum | solution.py:85
Sparse Core Ops, SparseCore 0:
  12.3 34.5 reduce-scatter.4
  191.8 110.3 reduce-scatter.6
  305.8 165.7 all-reduce.4
where the time goes:
time: 482 us; the launch traced here: 480 us
  waiting for transfers between devices  325 us (67%)
  local copies, waits for them, and re-layouts  54 us (11%)
  blocking collectives  47.1 us (10%)
  starting transfers between devices  25.1 us (5%)
  between operations  14 us (3%)
  matrix products  9.7 us (2%)
  other arithmetic  5.34 us (1%)
    psum x1, waiting for transfers between devices, on_device(): lax.psum(row_part.astype(jnp.bfloat16), 'tp')  168 us
    unnamed x4, waiting for transfers between devices  108 us
    psum x1, blocking collectives, norm_backward(): lax.psum((jnp.sum(values * values, axis=1), jnp.sum(scaled * values, axis...  33.1 us
    reduce_scatter x1, waiting for transfers between devices, on_device(): lax.psum_scatter(jnp.dot(x_rows, flat_w, preferred_element_type=jnp.float...  30 us
    scatter x1, local copies, waits for them, and re-layouts, on_device(): jnp.full((slot_count,), slots_dev, jnp.int32).at[target]  23 us
    unnamed x13, local copies, waits for them, and re-layouts  22.3 us
    all_to_all x1, waiting for transfers between devices, on_device(): lax.all_to_all(grad_slots, ('vis', 'dp'), split_axis=0, concat_axis=0, ti...  19.3 us
    all_gather x1, blocking collectives, on_device(): block_rows = lax.all_gather(grad_rows, 'dp', axis=0, tiled=True)  13.9 us
  transfers between devices with their start and end apart: 5, of which 4 were waited for; matrix products, arithmetic and copies ran while one was open for 7% of the time, Pallas kernels for 0%

commit v1 on v0

v1 whole, which is shorter than its diff:
```python
import functools

import jax
import jax.numpy as jnp
from jax import lax
from jax.experimental import pallas as pl
from jax.experimental.pallas import tpu as pltpu
from jax.sharding import PartitionSpec as P

MESH = pl.DeviceIdType.MESH
F32 = jnp.float32
BF16 = jnp.bfloat16
EPS = 1e-06
LANES = 128
CAP = 2
HALVES = 2


def remote(src, dst, send_sem, recv_sem, device):
    return pltpu.make_async_remote_copy(
        src_ref=src,
        dst_ref=dst,
        send_sem=send_sem,
        recv_sem=recv_sem,
        device_id=device,
        device_id_type=MESH,
    )


def kernel(
    sizes,
    x_ref,
    w_ref,
    gain_ref,
    pos_ref,
    cot_ref,
    fg_ref,
    wg_ref,
    pick,
    cot_cols,
    a2a_out,
    a2a_in,
    term,
    term_in,
    vals,
    scaled,
    stat_tile,
    stat_out,
    stat_in,
    grads,
    xt_plain,
    xt,
    own_part,
    sib_out,
    sib_in,
    right_out,
    right_in,
    left_out,
    left_in,
    row_part,
    row_in,
    cross_out,
    cross_in,
    fg_all,
    a2a_send,
    a2a_recv,
    term_send,
    term_recv,
    stat_send,
    stat_recv,
    grad_send,
    grad_recv,
    sib_send,
    sib_recv,
    right_send,
    right_recv,
    left_send,
    left_recv,
    row_send,
    row_recv,
    cross_send,
    cross_recv,
    full_send,
    full_recv,
):
    n_vis, n_tp, n_dp = sizes
    n_x = n_tp // 2
    n_z = n_vis // 2
    blocks = n_vis * n_dp
    rows = x_ref.shape[0]
    width = x_ref.shape[1]
    cols = w_ref.shape[1]
    per_block = rows // n_dp
    groups = cols // LANES
    slots_dev = cot_ref.shape[0]
    tile = CAP * groups
    total_cols = cols * n_tp
    half = cols // HALVES
    chunk = width // n_vis
    part_rows = rows // n_x
    part_cols = width // HALVES

    v = lax.axis_index("vis")
    t = lax.axis_index("tp")
    d = lax.axis_index("dp")
    z, core = v // 2, v % 2
    zh, xi = t // n_x, t % n_x
    me = v * n_dp + d

    def block_device(block):
        return {"vis": block // n_dp, "dp": block % n_dp}

    barrier = pltpu.get_barrier_semaphore()

    def greet(step, carry):
        pl.semaphore_signal(
            barrier, inc=1, device_id=block_device((me + step) % blocks), device_id_type=MESH
        )
        return carry

    for step in range(1, n_tp):
        pl.semaphore_signal(
            barrier, inc=1, device_id={"tp": (t + step) % n_tp}, device_id_type=MESH
        )
    lax.fori_loop(1, blocks, greet, 0)

    here = lax.broadcasted_iota(jnp.int32, (slots_dev, LANES), 0) + me * slots_dev
    block_at = jnp.full((slots_dev, LANES), -1, jnp.int32)
    for block in range(blocks):
        block_at = jnp.where(pos_ref[block : block + 1, :] == here, block, block_at)
    block_sub = jnp.broadcast_to(
        jnp.max(block_at.astype(F32), axis=1, keepdims=True), (slots_dev, LANES)
    )
    block_lane = block_sub.T
    first = lax.broadcasted_iota(jnp.int32, (LANES, LANES), 0)
    second = lax.broadcasted_iota(jnp.int32, (LANES, LANES), 1)
    earlier = jnp.where((block_sub == block_lane) & (first < second), 1.0, 0.0)
    rank = jnp.sum(earlier, axis=0, keepdims=True)
    slot = jnp.where(block_lane[0:1, :] < 0.0, -8192.0, block_lane[0:1, :] * CAP + rank)
    slot_row = slot.astype(jnp.int32) * groups
    out_row = lax.broadcasted_iota(jnp.int32, (blocks * tile, LANES), 0)
    for group in range(groups):
        span = pl.ds(group * LANES, LANES)
        pick[:, span] = jnp.where(out_row == slot_row + group, 1.0, 0.0).astype(BF16)
        cot_cols[pl.ds(group * slots_dev, slots_dev), :] = cot_ref[:, span]
    picked = jnp.dot(pick[...], cot_cols[...], preferred_element_type=F32).astype(BF16)
    a2a_out[...] = picked.reshape(blocks, tile, LANES)
    a2a_in[pl.ds(me, 1)] = a2a_out[pl.ds(me, 1)]

    pl.semaphore_wait(barrier, blocks - 1 + n_tp - 1)

    def send_slots(step, carry):
        block = (me + step) % blocks
        remote(
            a2a_out.at[block], a2a_in.at[me], a2a_send, a2a_recv, block_device(block)
        ).start()
        return carry

    lax.fori_loop(1, blocks, send_slots, 0)
    others = pl.ds(0, blocks - 1)
    a2a_all = remote(
        a2a_out.at[others], a2a_in.at[others], a2a_send, a2a_recv, block_device((me + 1) % blocks)
    )
    finish = [a2a_all.wait_send]

    order = [s for s in range(1, n_dp)]
    order.sort(key=lambda s: -min(s, n_dp - s))
    term_copies = []
    for h in range(HALVES):
        span = pl.ds(h * half, half)
        term[:, span] = jnp.dot(
            x_ref[...], w_ref[:, span], preferred_element_type=F32
        ).astype(BF16)
        for step in order:
            to = (d + step) % n_dp
            copy = remote(
                term.at[pl.ds(pl.multiple_of(to * per_block, 16), per_block), span],
                term_in.at[step - 1, :, span],
                term_send.at[h, step - 1],
                term_recv.at[h, step - 1],
                {"dp": to},
            )
            copy.start()
            term_copies.append(copy)
            finish.append(copy.wait_send)

    for start in range(0, width, LANES):
        xt_plain[pl.ds(start, LANES), :] = x_ref[:, pl.ds(start, LANES)].T
    for at in range(n_vis):
        xt[at % 2, pl.ds((at // 2) * chunk, chunk), :] = xt_plain[pl.ds(at * chunk, chunk), :]

    pos_lane = jnp.broadcast_to(pos_ref[pl.ds(me, 1), :], (LANES, LANES)).astype(F32)
    owner_lane = jnp.broadcast_to(
        pos_ref[pl.ds(me, 1), :] // slots_dev, (LANES, LANES)
    ).astype(F32)
    pos_sub = pos_lane.T
    owner_sub = owner_lane.T
    before = jnp.where((owner_sub == owner_lane) & (pos_lane < pos_sub), 1.0, 0.0)
    row_slot = owner_sub[:, 0:1] * CAP + jnp.sum(before, axis=1, keepdims=True)
    row_at = (row_slot[0:per_block] * groups).astype(jnp.int32)
    in_row = lax.broadcasted_iota(jnp.int32, (per_block, blocks * tile), 1)

    a2a_all.wait_recv()
    arrived = a2a_in[...].reshape(blocks * tile, LANES)
    for group in range(groups):
        span = pl.ds(group * LANES, LANES)
        select = jnp.where(in_row == row_at + group, 1.0, 0.0).astype(BF16)
        scaled[:, span] = (
            jnp.dot(select, arrived, preferred_element_type=F32) * gain_ref[:, span]
        )

    for copy in term_copies:
        copy.wait_recv()
    mine = pl.ds(pl.multiple_of(d * per_block, 16), per_block)
    total = term[mine, :].astype(F32)
    for step in range(1, n_dp):
        total = total + term_in[step - 1].astype(F32)
    value = total.astype(BF16).astype(F32)
    vals[...] = value
    square = jnp.sum(value * value, axis=1, keepdims=True)
    dotted = jnp.sum(scaled[...] * value, axis=1, keepdims=True)

    lane = lax.broadcasted_iota(jnp.int32, (per_block, LANES), 1)
    stat_tile[...] = jnp.zeros_like(stat_tile)
    stat_tile[0:per_block, :] = jnp.where(lane == 0, square, jnp.where(lane == 1, dotted, 0.0))
    stat_out[...] = stat_tile[...].T[0:8, :]
    stat_in[pl.ds(t, 1)] = stat_out[...].reshape(1, 8, LANES)
    stat_copies = []
    for step in sorted(range(1, n_tp), key=lambda s: -(s == n_x)):
        copy = remote(
            stat_out,
            stat_in.at[t],
            stat_send.at[step - 1],
            stat_recv.at[step - 1],
            {"tp": (t + step) % n_tp},
        )
        copy.start()
        stat_copies.append(copy)
        finish.append(copy.wait_send)
    for copy in stat_copies:
        copy.wait_recv()
    sums = stat_in[0]
    for at in range(1, n_tp):
        sums = sums + stat_in[at]
    inverse = lax.rsqrt(sums[0:1, :] / total_cols + EPS)
    factor = inverse * inverse * inverse * (sums[1:2, :] / total_cols)
    sub = lax.broadcasted_iota(jnp.int32, (LANES, LANES), 0)
    spread = jnp.where(sub == 0, inverse, jnp.where(sub == 1, factor, 0.0)).T
    inverse_col = spread[0:per_block, 0:1]
    factor_col = spread[0:per_block, 1:2]

    grad_copies = []
    for h in range(HALVES):
        span = pl.ds(h * half, half)
        grads[mine, span] = (
            inverse_col * scaled[:, span] - factor_col * vals[:, span]
        ).astype(BF16)
        copies = []
        for step in order:
            copy = remote(
                grads.at[mine, span],
                grads.at[mine, span],
                grad_send.at[h, step - 1],
                grad_recv.at[h, step - 1],
                {"dp": (d + step) % n_dp},
            )
            copy.start()
            finish.append(copy.wait_send)
            source = (d + n_dp - step) % n_dp
            landed = grads.at[
                pl.ds(pl.multiple_of(source * per_block, 16), per_block), span
            ]
            copies.append(
                remote(
                    landed,
                    landed,
                    grad_send.at[h, step - 1],
                    grad_recv.at[h, step - 1],
                    {"dp": (d + step) % n_dp},
                )
            )
        grad_copies.append(copies)

    sib_copies = []
    for h in range(HALVES):
        span = pl.ds(h * half, half)
        for copy in grad_copies[h]:
            copy.wait_recv()
        sib_out[h] = jnp.dot(
            xt[1 - core], grads[:, span], preferred_element_type=F32
        ).astype(BF16)
        copy = remote(
            sib_out.at[h],
            sib_in.at[h],
            sib_send.at[h],
            sib_recv.at[h],
            {"vis": v + 1 - 2 * core},
        )
        copy.start()
        sib_copies.append(copy)
        finish.append(copy.wait_send)
        own_part[h] = jnp.dot(xt[core], grads[:, span], preferred_element_type=F32).astype(BF16)

    x_order = sorted(range(1, n_x), key=lambda s: -min(s, n_x - s))

    def feature_products(f):
        span = pl.ds(f * part_cols, part_cols)
        row_part[:, span] = lax.dot_general(
            grads[...], w_ref[span, :], (((1,), (1,)), ((), ())), preferred_element_type=F32
        ).astype(BF16)
        copies = []
        for step in x_order:
            to = (xi + step) % n_x
            copy = remote(
                row_part.at[pl.ds(pl.multiple_of(to * part_rows, 16), part_rows), span],
                row_in.at[step - 1, :, span],
                row_send.at[f, step - 1],
                row_recv.at[f, step - 1],
                {"tp": zh * n_x + to},
            )
            copy.start()
            copies.append(copy)
            finish.append(copy.wait_send)
        return copies

    part = pl.ds(pl.multiple_of(xi * part_rows, 16), part_rows)

    def feature_cross(f, copies):
        span = pl.ds(f * part_cols, part_cols)
        for copy in copies:
            copy.wait_recv()
        summed = row_part[part, span].astype(F32)
        for step in range(1, n_x):
            summed = summed + row_in[step - 1, :, span].astype(F32)
        cross_out[f] = summed.astype(BF16)
        copy = remote(
            cross_out.at[f],
            cross_in.at[f],
            cross_send.at[f],
            cross_recv.at[f],
            {"tp": (t + n_x) % n_tp},
        )
        copy.start()
        finish.append(copy.wait_send)
        return copy

    def feature_spread(f, copy):
        span = pl.ds(f * part_cols, part_cols)
        copy.wait_recv()
        fg_all[part, span] = (cross_out[f].astype(F32) + cross_in[f].astype(F32)).astype(BF16)
        copies = []
        for step in x_order:
            send = remote(
                fg_all.at[part, span],
                fg_all.at[part, span],
                full_send.at[f, step - 1],
                full_recv.at[f, step - 1],
                {"tp": zh * n_x + (xi + step) % n_x},
            )
            send.start()
            finish.append(send.wait_send)
            source = (xi + n_x - step) % n_x
            landed = fg_all.at[
                pl.ds(pl.multiple_of(source * part_rows, 16), part_rows), span
            ]
            copies.append(
                remote(
                    landed,
                    landed,
                    full_send.at[f, step - 1],
                    full_recv.at[f, step - 1],
                    {"tp": zh * n_x + (xi + step) % n_x},
                )
            )
        return copies

    def line_copy(out, into, send_sem, recv_sem, at, h, to):
        return remote(
            out.at[at, h], into.at[at, h], send_sem.at[at, h], recv_sem.at[at, h], {"vis": to}
        )

    right = jnp.minimum(v + 2, n_vis - 2 + core)
    left = jnp.maximum(v - 2, core)

    def pair_sum(at, h):
        span = pl.ds(pl.multiple_of(at * chunk, 16), chunk)
        return own_part[h, span, :].astype(F32) + sib_in[h, span, :].astype(F32)

    def line_step(tau):
        for h in range(HALVES):

            @pl.when((z <= tau) & (z < n_z - 1) & (tau < n_z - 1))
            def _():
                at = n_z - 1 - tau + z
                copy = line_copy(right_out, right_in, right_send, right_recv, at, h, right)

                @pl.when(z > 0)
                def _():
                    copy.wait_recv()
                    right_out[at, h] = (
                        pair_sum(at, h) + right_in[at, h].astype(F32)
                    ).astype(BF16)

                @pl.when(z == 0)
                def _():
                    right_out[at, h] = pair_sum(at, h).astype(BF16)

                copy.start()

            @pl.when((n_z - 1 - z <= tau) & (z > 0) & (tau < n_z - 1))
            def _():
                at = tau - (n_z - 1 - z)
                copy = line_copy(left_out, left_in, left_send, left_recv, at, h, left)

                @pl.when(z < n_z - 1)
                def _():
                    copy.wait_recv()
                    left_out[at, h] = (
                        pair_sum(at, h) + left_in[at, h].astype(F32)
                    ).astype(BF16)

                @pl.when(z == n_z - 1)
                def _():
                    left_out[at, h] = pair_sum(at, h).astype(BF16)

                copy.start()

    def line_last():
        for h in range(HALVES):
            span = pl.ds(h * half, half)
            from_left = line_copy(right_out, right_in, right_send, right_recv, z, h, right)
            from_right = line_copy(left_out, left_in, left_send, left_recv, z, h, left)

            @pl.when(z > 0)
            def _():
                from_left.wait_recv()

            @pl.when(z < n_z - 1)
            def _():
                from_right.wait_recv()

            @pl.when(z == 0)
            def _():
                wg_ref[:, span] = (pair_sum(z, h) + left_in[z, h].astype(F32)).astype(BF16)

            @pl.when(z == n_z - 1)
            def _():
                wg_ref[:, span] = (pair_sum(z, h) + right_in[z, h].astype(F32)).astype(BF16)

            @pl.when((z > 0) & (z < n_z - 1))
            def _():
                wg_ref[:, span] = (
                    pair_sum(z, h) + right_in[z, h].astype(F32) + left_in[z, h].astype(F32)
                ).astype(BF16)

    def line_sent():
        for h in range(HALVES):

            def right_done(at, carry):
                line_copy(right_out, right_in, right_send, right_recv, at, h, right).wait_send()
                return carry

            def left_done(at, carry):
                line_copy(left_out, left_in, left_send, left_recv, at, h, left).wait_send()
                return carry

            lax.fori_loop(z + 1, n_z, right_done, 0)
            lax.fori_loop(0, z, left_done, 0)

    row_copies = [feature_products(f) for f in range(HALVES)]
    for copy in sib_copies:
        copy.wait_recv()
    line_step(0)
    line_step(1)
    cross = [feature_cross(0, row_copies[0])]
    line_step(2)
    cross.append(feature_cross(1, row_copies[1]))
    for tau in range(3, n_z - 2):
        line_step(tau)
    spread_copies = feature_spread(0, cross[0])
    for tau in range(max(3, n_z - 2), n_z - 1):
        line_step(tau)
    spread_copies += feature_spread(1, cross[1])
    line_last()
    for copy in spread_copies:
        copy.wait_recv()
    fg_ref[...] = fg_all[...]
    line_sent()
    for wait in finish:
        wait()


def on_device(features, merge_weight, gain, positions, cotangent):
    rows, sub_count, width = features.shape
    cols = merge_weight.shape[2]
    n_vis, n_tp, n_dp = (lax.axis_size(name) for name in ("vis", "tp", "dp"))
    blocks = n_vis * n_dp
    per_block = rows // n_dp
    slots_dev = cotangent.shape[0]
    groups = cols // LANES
    tile = CAP * groups
    n_x, n_z = n_tp // 2, n_vis // 2
    half = cols // HALVES
    chunk = width // n_vis
    share = width // 2
    part_rows = rows // n_x
    part_cols = width // HALVES
    table = jnp.pad(
        positions.reshape(blocks, per_block), ((0, 0), (0, LANES - per_block)), constant_values=-1
    )
    vmem = pl.BlockSpec(memory_space=pltpu.VMEM)
    dma = pltpu.SemaphoreType.DMA
    feature_grad, weight_grad = pl.pallas_call(
        functools.partial(kernel, (n_vis, n_tp, n_dp)),
        out_shape=(
            jax.ShapeDtypeStruct((rows, width), BF16),
            jax.ShapeDtypeStruct((chunk, cols), BF16),
        ),
        in_specs=[vmem] * 5,
        out_specs=(vmem, vmem),
        scratch_shapes=[
            pltpu.VMEM((blocks * tile, groups * slots_dev), BF16),
            pltpu.VMEM((groups * slots_dev, LANES), BF16),
            pltpu.VMEM((blocks, tile, LANES), BF16),
            pltpu.VMEM((blocks, tile, LANES), BF16),
            pltpu.VMEM((rows, cols), BF16),
            pltpu.VMEM((n_dp - 1, per_block, cols), BF16),
            pltpu.VMEM((per_block, cols), F32),
            pltpu.VMEM((per_block, cols), F32),
            pltpu.VMEM((LANES, LANES), F32),
            pltpu.VMEM((8, LANES), F32),
            pltpu.VMEM((n_tp, 8, LANES), F32),
            pltpu.VMEM((rows, cols), BF16),
            pltpu.VMEM((width, rows), BF16),
            pltpu.VMEM((2, share, rows), BF16),
            pltpu.VMEM((HALVES, share, half), BF16),
            pltpu.VMEM((HALVES, share, half), BF16),
            pltpu.VMEM((HALVES, share, half), BF16),
            pltpu.VMEM((n_z, HALVES, chunk, half), BF16),
            pltpu.VMEM((n_z, HALVES, chunk, half), BF16),
            pltpu.VMEM((n_z, HALVES, chunk, half), BF16),
            pltpu.VMEM((n_z, HALVES, chunk, half), BF16),
            pltpu.VMEM((rows, width), BF16),
            pltpu.VMEM((n_x - 1, part_rows, width), BF16),
            pltpu.VMEM((HALVES, part_rows, part_cols), BF16),
            pltpu.VMEM((HALVES, part_rows, part_cols), BF16),
            pltpu.VMEM((rows, width), BF16),
            dma,
            dma,
            dma((HALVES, n_dp - 1)),
            dma((HALVES, n_dp - 1)),
            dma((n_tp - 1,)),
            dma((n_tp - 1,)),
            dma((HALVES, n_dp - 1)),
            dma((HALVES, n_dp - 1)),
            dma((HALVES,)),
            dma((HALVES,)),
            dma((n_z, HALVES)),
            dma((n_z, HALVES)),
            dma((n_z, HALVES)),
            dma((n_z, HALVES)),
            dma((HALVES, n_x - 1)),
            dma((HALVES, n_x - 1)),
            dma((HALVES,)),
            dma((HALVES,)),
            dma((HALVES, n_x - 1)),
            dma((HALVES, n_x - 1)),
        ],
        compiler_params=pltpu.CompilerParams(
            collective_id=0, has_side_effects=True, vmem_limit_bytes=56 << 20
        ),
        cost_estimate=pl.CostEstimate(
            flops=6 * rows * width * cols, bytes_accessed=6 * width * cols, transcendentals=LANES
        ),
    )(
        features.reshape(rows, width),
        merge_weight.reshape(width, cols),
        gain.reshape(1, cols),
        table,
        cotangent,
    )
    return (feature_grad.reshape(features.shape), weight_grad.reshape(1, chunk, cols))


def solution(mesh):
    return jax.shard_map(
        on_device,
        mesh=mesh,
        in_specs=(P("vis", "dp", None), P("dp", None, "tp"), P("tp"), P(), P(("vis", "dp"), "tp")),
        out_specs=(P("vis", "dp", None), P("dp", "vis", "tp")),
        check_vma=False,
    )
```

time: 482 us -> 115 us (0.24)
  the two profiles are of different devices: /device:TPU:6 before, /device:TPU:32 now
where the time goes in v1:
time: 115 us
  Pallas kernels  109 us (95%)
  local copies, waits for them, and re-layouts  5.24 us (5%)
    pallas_call x1, Pallas kernels, on_device(): pl.pallas_call(functools.partial(kernel, (n_vis, n_tp, n_dp)), out_shape=...  109 us
    unnamed x2, local copies, waits for them, and re-layouts  3.8 us

profile of v1, /device:TPU:32, one launch (start us, length us, event | category | flops | bytes accessed | tf_op | source)
XLA Modules:
  0.0 114.7 jit_solution(18159614801708964800)
XLA Ops:
  0.6 0.8 reshape.25
  1.4 0.6 pad.4.pos_ref
  2.1 108.9 %shard_map.68 = (bf16[384,1280]{1,0:T(8,128)(2,1)}, bf16[80,1024]{1,0:T(8,128)(2,1)}) custom-call(bf16[384,1280]{1,0:T(8,128)(2,1)} %bitcast.8, bf16[1280,1024]{1,0:T(8,128)(2,1)} %bitcast.7, f32[1,1024]{1,0:T(1,128)} %bitcast.9, s32[64,128]{1,0:T(8,128)} %pad.4.pos_ref, bf16[128,1024]{1,0:T(8,128)(2,1)} %cot_ref.1), custom_call_target="tpu_custom_call" | custom-call | flops 3019898880 | bytes 7864320 | tf_op jit(solution)/shard_map/pallas_call | solution.py:513
  110.9 2.2 %copy.9 = bf16[384,1,1280]{2,0,1:T(8,128)(2,1)} copy(bf16[384,1,1280]{2,0,1:T(8,128)(2,1)} %bitcast.5) | data formatting | bytes 1966080
  113.1 1.6 %copy.10 = bf16[1,80,1024]{2,1,0:T(8,128)(2,1)} copy(bf16[1,80,1024]{2,1,0:T(8,128)(2,1)} %bitcast.6) | data formatting | bytes 327680

commit v2 on v1

--- a/solution.py
+++ b/solution.py
@@ -14,6 +14,9 @@
 LANES = 128
 CAP = 2
 HALVES = 2
+GROUPS = ((0, 16), (16, 16), (32, 32), (64, 32))
+PIECES = 4
+N_GROUPS = len(GROUPS)
 
 
 def remote(src, dst, send_sem, recv_sem, device):
@@ -50,6 +53,7 @@
     grads,
     xt_plain,
     xt,
+    wt,
     own_part,
     sib_out,
     sib_in,
@@ -97,8 +101,6 @@
     total_cols = cols * n_tp
     half = cols // HALVES
     chunk = width // n_vis
-    part_rows = rows // n_x
-    part_cols = width // HALVES
 
     v = lax.axis_index("vis")
     t = lax.axis_index("tp")
@@ -126,8 +128,10 @@
 
     here = lax.broadcasted_iota(jnp.int32, (slots_dev, LANES), 0) + me * slots_dev
     block_at = jnp.full((slots_dev, LANES), -1, jnp.int32)
-    for block in range(blocks):
-        block_at = jnp.where(pos_ref[block : block + 1, :] == here, block, block_at)
+    for line in range(pos_ref.shape[0]):
+        block_at = jnp.where(pos_ref[line : line + 1, :] == here, line, block_at)
+    lane_at = lax.broadcasted_iota(jnp.int32, (slots_dev, LANES), 1)
+    block_at = jnp.where(block_at < 0, -1, (block_at * LANES + lane_at) // per_block)
     block_sub = jnp.broadcast_to(
         jnp.max(block_at.astype(F32), axis=1, keepdims=True), (slots_dev, LANES)
     )
@@ -189,12 +193,23 @@
     for at in range(n_vis):
         xt[at % 2, pl.ds((at // 2) * chunk, chunk), :] = xt_plain[pl.ds(at * chunk, chunk), :]
 
-    pos_lane = jnp.broadcast_to(pos_ref[pl.ds(me, 1), :], (LANES, LANES)).astype(F32)
-    owner_lane = jnp.broadcast_to(
-        pos_ref[pl.ds(me, 1), :] // slots_dev, (LANES, LANES)
-    ).astype(F32)
-    pos_sub = pos_lane.T
-    owner_sub = owner_lane.T
+    for start in range(0, cols, LANES):
+        wt[pl.ds(start, LANES), :] = w_ref[:, pl.ds(start, LANES)].T
+
+    flat = lax.broadcasted_iota(jnp.int32, (LANES, LANES), 0) + me * per_block
+    line_first = (me * per_block) // LANES
+    line_next = jnp.minimum(line_first + 1, pos_ref.shape[0] - 1)
+    line_pos = jnp.where(
+        flat // LANES == line_first, pos_ref[pl.ds(line_first, 1), :], pos_ref[pl.ds(line_next, 1), :]
+    )
+    row_pos = jnp.sum(
+        jnp.where(flat % LANES == second, line_pos, 0).astype(F32), axis=1, keepdims=True
+    )
+    row_pos = jnp.where(first[:, 0:1] < per_block, row_pos, -1.0)
+    pos_sub = jnp.broadcast_to(row_pos, (LANES, LANES))
+    owner_sub = jnp.floor(pos_sub / slots_dev)
+    pos_lane = pos_sub.T
+    owner_lane = owner_sub.T
     before = jnp.where((owner_sub == owner_lane) & (pos_lane < pos_sub), 1.0, 0.0)
     row_slot = owner_sub[:, 0:1] * CAP + jnp.sum(before, axis=1, keepdims=True)
     row_at = (row_slot[0:per_block] * groups).astype(jnp.int32)
@@ -250,42 +265,37 @@
     factor_col = spread[0:per_block, 1:2]
 
     grad_copies = []
-    for h in range(HALVES):
+    grad_sent = []
+
+    def send_grads(g):
+        at, size = GROUPS[g]
+        inside = pl.ds(at, size)
+        group = pl.ds(pl.multiple_of(d * per_block + at, 16), size)
+        grads[group, :] = (
+            inverse_col[at : at + size] * scaled[inside, :]
+            - factor_col[at : at + size] * vals[inside, :]
+        ).astype(BF16)
+        arrivals, sent = [], []
+        for step in order:
+            to = {"dp": (d + step) % n_dp}
+            sems = grad_send.at[g, step - 1], grad_recv.at[g, step - 1]
+            copy = remote(grads.at[group], grads.at[group], *sems, to)
+            copy.start()
+            sent.append(copy.wait_send)
+            source = (d + n_dp - step) % n_dp
+            landed = grads.at[pl.ds(pl.multiple_of(source * per_block + at, 16), size)]
+            arrivals.append(remote(landed, landed, *sems, to))
+        grad_copies.append(arrivals)
+        grad_sent.append(sent)
+
+    def grads_gone(g):
+        for wait in grad_sent[g]:
+            wait()
+
+    sib_copies = []
+
+    def share_out(h):
         span = pl.ds(h * half, half)
-        grads[mine, span] = (
-            inverse_col * scaled[:, span] - factor_col * vals[:, span]
-        ).astype(BF16)
-        copies = []
-        for step in order:
-            copy = remote(
-                grads.at[mine, span],
-                grads.at[mine, span],
-                grad_send.at[h, step - 1],
-                grad_recv.at[h, step - 1],
-                {"dp": (d + step) % n_dp},
-            )
-            copy.start()
-            finish.append(copy.wait_send)
-            source = (d + n_dp - step) % n_dp
-            landed = grads.at[
-                pl.ds(pl.multiple_of(source * per_block, 16), per_block), span
-            ]
-            copies.append(
-                remote(
-                    landed,
-                    landed,
-                    grad_send.at[h, step - 1],
-                    grad_recv.at[h, step - 1],
-                    {"dp": (d + step) % n_dp},
-                )
-            )
-        grad_copies.append(copies)
-
-    sib_copies = []
-    for h in range(HALVES):
-        span = pl.ds(h * half, half)
-        for copy in grad_copies[h]:
-            copy.wait_recv()
         sib_out[h] = jnp.dot(
             xt[1 - core], grads[:, span], preferred_element_type=F32
         ).astype(BF16)
@@ -299,23 +309,31 @@
         copy.start()
         sib_copies.append(copy)
         finish.append(copy.wait_send)
+
+    def share_own(h):
+        span = pl.ds(h * half, half)
         own_part[h] = jnp.dot(xt[core], grads[:, span], preferred_element_type=F32).astype(BF16)
 
     x_order = sorted(range(1, n_x), key=lambda s: -min(s, n_x - s))
 
-    def feature_products(f):
-        span = pl.ds(f * part_cols, part_cols)
-        row_part[:, span] = lax.dot_general(
-            grads[...], w_ref[span, :], (((1,), (1,)), ((), ())), preferred_element_type=F32
+    def feature_products(g):
+        at, size = GROUPS[g]
+        for copy in grad_copies[g]:
+            copy.wait_recv()
+        group = jnp.concatenate(
+            [grads[pl.ds(block * per_block + at, size), :] for block in range(n_dp)], axis=0
+        )
+        row_part[pl.ds(n_dp * at, n_dp * size), :] = jnp.dot(
+            group, wt[...], preferred_element_type=F32
         ).astype(BF16)
         copies = []
         for step in x_order:
             to = (xi + step) % n_x
             copy = remote(
-                row_part.at[pl.ds(pl.multiple_of(to * part_rows, 16), part_rows), span],
-                row_in.at[step - 1, :, span],
-                row_send.at[f, step - 1],
-                row_recv.at[f, step - 1],
+                row_part.at[pl.ds(pl.multiple_of(n_dp * at + to * size, 16), size)],
+                row_in.at[step - 1, pl.ds(at, size)],
+                row_send.at[g, step - 1],
+                row_recv.at[g, step - 1],
                 {"tp": zh * n_x + to},
             )
             copy.start()
@@ -323,55 +341,46 @@
             finish.append(copy.wait_send)
         return copies
 
-    part = pl.ds(pl.multiple_of(xi * part_rows, 16), part_rows)
-
-    def feature_cross(f, copies):
-        span = pl.ds(f * part_cols, part_cols)
+    def feature_cross(g, copies):
+        at, size = GROUPS[g]
+        inside = pl.ds(at, size)
         for copy in copies:
             copy.wait_recv()
-        summed = row_part[part, span].astype(F32)
+        summed = row_part[
+            pl.ds(pl.multiple_of(n_dp * at + xi * size, 16), size), :
+        ].astype(F32)
         for step in range(1, n_x):
-            summed = summed + row_in[step - 1, :, span].astype(F32)
-        cross_out[f] = summed.astype(BF16)
+            summed = summed + row_in[step - 1, inside, :].astype(F32)
+        cross_out[inside, :] = summed.astype(BF16)
         copy = remote(
-            cross_out.at[f],
-            cross_in.at[f],
-            cross_send.at[f],
-            cross_recv.at[f],
+            cross_out.at[inside],
+            cross_in.at[inside],
+            cross_send.at[g],
+            cross_recv.at[g],
             {"tp": (t + n_x) % n_tp},
         )
         copy.start()
         finish.append(copy.wait_send)
         return copy
 
-    def feature_spread(f, copy):
-        span = pl.ds(f * part_cols, part_cols)
+    def feature_spread(g, copy):
+        at, size = GROUPS[g]
+        inside = pl.ds(at, size)
         copy.wait_recv()
-        fg_all[part, span] = (cross_out[f].astype(F32) + cross_in[f].astype(F32)).astype(BF16)
+        place = pl.ds(pl.multiple_of(xi * per_block + at, 16), size)
+        fg_all[place, :] = (
+            cross_out[inside, :].astype(F32) + cross_in[inside, :].astype(F32)
+        ).astype(BF16)
         copies = []
         for step in x_order:
-            send = remote(
-                fg_all.at[part, span],
-                fg_all.at[part, span],
-                full_send.at[f, step - 1],
-                full_recv.at[f, step - 1],
-                {"tp": zh * n_x + (xi + step) % n_x},
-            )
+            to = {"tp": zh * n_x + (xi + step) % n_x}
+            sems = full_send.at[g, step - 1], full_recv.at[g, step - 1]
+            send = remote(fg_all.at[place], fg_all.at[place], *sems, to)
             send.start()
             finish.append(send.wait_send)
             source = (xi + n_x - step) % n_x
-            landed = fg_all.at[
-                pl.ds(pl.multiple_of(source * part_rows, 16), part_rows), span
-            ]
-            copies.append(
-                remote(
-                    landed,
-                    landed,
-                    full_send.at[f, step - 1],
-                    full_recv.at[f, step - 1],
-                    {"tp": zh * n_x + (xi + step) % n_x},
-                )
-            )
+            landed = fg_all.at[pl.ds(pl.multiple_of(source * per_block + at, 16), size)]
+            copies.append(remote(landed, landed, *sems, to))
         return copies
 
     def line_copy(out, into, send_sem, recv_sem, at, h, to):
@@ -467,27 +476,64 @@
             lax.fori_loop(z + 1, n_z, right_done, 0)
             lax.fori_loop(0, z, left_done, 0)
 
-    row_copies = [feature_products(f) for f in range(HALVES)]
+    send_grads(0)
+    send_grads(1)
+    row_copies = [feature_products(0)]
+    grads_gone(0)
+    send_grads(2)
+    row_copies.append(feature_products(1))
+    grads_gone(1)
+    send_grads(3)
+    cross = [feature_cross(0, row_copies[0])]
+    row_copies.append(feature_products(2))
+    cross.append(feature_cross(1, row_copies[1]))
+    row_copies.append(feature_products(3))
+    share_out(0)
+    share_out(1)
+    cross.append(feature_cross(2, row_copies[2]))
+    share_own(0)
+    share_own(1)
     for copy in sib_copies:
         copy.wait_recv()
+    cross.append(feature_cross(3, row_copies[3]))
+    spread_copies = feature_spread(0, cross[0])
     line_step(0)
+    spread_copies += feature_spread(1, cross[1])
     line_step(1)
-    cross = [feature_cross(0, row_copies[0])]
     line_step(2)
-    cross.append(feature_cross(1, row_copies[1]))
-    for tau in range(3, n_z - 2):
-        line_step(tau)
-    spread_copies = feature_spread(0, cross[0])
-    for tau in range(max(3, n_z - 2), n_z - 1):
-        line_step(tau)
-    spread_copies += feature_spread(1, cross[1])
+    spread_copies += feature_spread(2, cross[2])
+    line_step(3)
+    spread_copies += feature_spread(3, cross[3])
+    line_step(4)
+    line_step(5)
+    line_step(6)
     line_last()
     for copy in spread_copies:
         copy.wait_recv()
     fg_ref[...] = fg_all[...]
     line_sent()
+    grads_gone(2)
+    grads_gone(3)
     for wait in finish:
         wait()
+
+
+def hand_on(fg_in, wg_in, fg_ref, wg_ref, fg_held, wg_held, sems_in, sems_out):
+    pieces = sems_in.shape[0] - 1
+    size = fg_in.shape[0] // pieces
+    spans = [pl.ds(at * size, size) for at in range(pieces)]
+    sources = [fg_in.at[span] for span in spans] + [wg_in]
+    held = [fg_held.at[span] for span in spans] + [wg_held]
+    targets = [fg_ref.at[span] for span in spans] + [wg_ref]
+    into = [pltpu.make_async_copy(a, b, sems_in.at[k]) for k, (a, b) in enumerate(zip(sources, held))]
+    out = [pltpu.make_async_copy(a, b, sems_out.at[k]) for k, (a, b) in enumerate(zip(held, targets))]
+    for copy in into:
+        copy.start()
+    for first, second in zip(into, out):
+        first.wait()
+        second.start()
+    for copy in out:
+        copy.wait()
 
 
 def on_device(features, merge_weight, gain, positions, cotangent):
@@ -503,11 +549,6 @@
     half = cols // HALVES
     chunk = width // n_vis
     share = width // 2
-    part_rows = rows // n_x
-    part_cols = width // HALVES
-    table = jnp.pad(
-        positions.reshape(blocks, per_block), ((0, 0), (0, LANES - per_block)), constant_values=-1
-    )
     vmem = pl.BlockSpec(memory_space=pltpu.VMEM)
     dma = pltpu.SemaphoreType.DMA
     feature_grad, weight_grad = pl.pallas_call(
@@ -533,6 +574,7 @@
             pltpu.VMEM((rows, cols), BF16),
             pltpu.VMEM((width, rows), BF16),
             pltpu.VMEM((2, share, rows), BF16),
+            pltpu.VMEM((cols, width), BF16),
             pltpu.VMEM((HALVES, share, half), BF16),
             pltpu.VMEM((HALVES, share, half), BF16),
             pltpu.VMEM((HALVES, share, half), BF16),
@@ -541,9 +583,9 @@
             pltpu.VMEM((n_z, HALVES, chunk, half), BF16),
             pltpu.VMEM((n_z, HALVES, chunk, half), BF16),
             pltpu.VMEM((rows, width), BF16),
-            pltpu.VMEM((n_x - 1, part_rows, width), BF16),
-            pltpu.VMEM((HALVES, part_rows, part_cols), BF16),
-            pltpu.VMEM((HALVES, part_rows, part_cols), BF16),
+            pltpu.VMEM((n_x - 1, per_block, width), BF16),
+            pltpu.VMEM((per_block, width), BF16),
+            pltpu.VMEM((per_block, width), BF16),
             pltpu.VMEM((rows, width), BF16),
             dma,
             dma,
@@ -551,20 +593,20 @@
             dma((HALVES, n_dp - 1)),
             dma((n_tp - 1,)),
             dma((n_tp - 1,)),
-            dma((HALVES, n_dp - 1)),
-            dma((HALVES, n_dp - 1)),
+            dma((N_GROUPS, n_dp - 1)),
+            dma((N_GROUPS, n_dp - 1)),
             dma((HALVES,)),
             dma((HALVES,)),
             dma((n_z, HALVES)),
             dma((n_z, HALVES)),
             dma((n_z, HALVES)),
             dma((n_z, HALVES)),
-            dma((HALVES, n_x - 1)),
-            dma((HALVES, n_x - 1)),
-            dma((HALVES,)),
-            dma((HALVES,)),
-            dma((HALVES, n_x - 1)),
-            dma((HALVES, n_x - 1)),
+            dma((N_GROUPS, n_x - 1)),
+            dma((N_GROUPS, n_x - 1)),
+            dma((N_GROUPS,)),
+            dma((N_GROUPS,)),
+            dma((N_GROUPS, n_x - 1)),
+            dma((N_GROUPS, n_x - 1)),
         ],
         compiler_params=pltpu.CompilerParams(
             collective_id=0, has_side_effects=True, vmem_limit_bytes=56 << 20
@@ -576,9 +618,26 @@
         features.reshape(rows, width),
         merge_weight.reshape(width, cols),
         gain.reshape(1, cols),
-        table,
+        positions.reshape(-1, LANES),
         cotangent,
     )
+    anywhere = pl.BlockSpec(memory_space=pl.ANY)
+    feature_grad, weight_grad = pl.pallas_call(
+        hand_on,
+        out_shape=(
+            jax.ShapeDtypeStruct((rows, width), BF16),
+            jax.ShapeDtypeStruct((chunk, cols), BF16),
+        ),
+        in_specs=[anywhere] * 2,
+        out_specs=(anywhere, anywhere),
+        scratch_shapes=[
+            pltpu.VMEM((rows, width), BF16),
+            pltpu.VMEM((chunk, cols), BF16),
+            dma((PIECES + 1,)),
+            dma((PIECES + 1,)),
+        ],
+        compiler_params=pltpu.CompilerParams(vmem_limit_bytes=60 << 20),
+    )(feature_grad, weight_grad)
     return (feature_grad.reshape(features.shape), weight_grad.reshape(1, chunk, cols))
 
 

time: 115 us -> 106 us (0.922)
  the two profiles are of different devices: /device:TPU:32 before, /device:TPU:6 now
where the time goes in v2:
time: 106 us
  Pallas kernels  106 us (100%)
    pallas_call x1, Pallas kernels, on_device(): pl.pallas_call(functools.partial(kernel, (n_vis, n_tp, n_dp)), out_shape=...  104 us
    pallas_call x1, Pallas kernels, on_device(): pl.pallas_call(hand_on, out_shape=(jax.ShapeDtypeStruct((rows, width), BF...  2.14 us

profile of v2, /device:TPU:6, one launch (start us, length us, event | category | flops | bytes accessed | tf_op | source)
XLA Modules:
  0.0 106.3 jit_solution(15712219374238826433)
XLA Ops:
  0.6 103.6 %shard_map.68 = (bf16[384,1280]{1,0:T(8,128)(2,1)}, bf16[80,1024]{1,0:T(8,128)(2,1)}) custom-call(bf16[384,1280]{1,0:T(8,128)(2,1)} %bitcast.7, bf16[1280,1024]{1,0:T(8,128)(2,1)} %bitcast.6, f32[1,1024]{1,0:T(1,128)} %bitcast.11, s32[48,128]{1,0:T(8,128)} %bitcast.10, bf16[128,1024]{1,0:T(8,128)(2,1)} %cot_ref.1), custom_call_target="tpu_custom_call" | custom-call | flops 3019898880 | bytes 7864320 | tf_op jit(solution)/shard_map/pallas_call | solution.py:554
  104.2 2.1 %shard_map.69 = (bf16[384,1280]{1,0:T(8,128)(2,1)}, bf16[80,1024]{1,0:T(8,128)(2,1)}) custom-call(bf16[384,1280]{1,0:T(8,128)(2,1)} %get-tuple-element.6.fg_in, bf16[80,1024]{1,0:T(8,128)(2,1)} %get-tuple-element.7.wg_in), custom_call_target="tpu_custom_call" | custom-call | tf_op jit(solution)/shard_map/pallas_call | solution.py:625

commit v3 on v2

--- a/solution.py
+++ b/solution.py
@@ -14,9 +14,9 @@
 LANES = 128
 CAP = 2
 HALVES = 2
-GROUPS = ((0, 16), (16, 16), (32, 32), (64, 32))
+STRIP = 16
+SENDS = 4
 PIECES = 4
-N_GROUPS = len(GROUPS)
 
 
 def remote(src, dst, send_sem, recv_sem, device):
@@ -39,8 +39,7 @@
     cot_ref,
     fg_ref,
     wg_ref,
-    pick,
-    cot_cols,
+    slots_wide,
     a2a_out,
     a2a_in,
     term,
@@ -141,14 +140,15 @@
     earlier = jnp.where((block_sub == block_lane) & (first < second), 1.0, 0.0)
     rank = jnp.sum(earlier, axis=0, keepdims=True)
     slot = jnp.where(block_lane[0:1, :] < 0.0, -8192.0, block_lane[0:1, :] * CAP + rank)
-    slot_row = slot.astype(jnp.int32) * groups
-    out_row = lax.broadcasted_iota(jnp.int32, (blocks * tile, LANES), 0)
+    slot_row = slot.astype(jnp.int32)
+    pick = jnp.where(
+        lax.broadcasted_iota(jnp.int32, (blocks * CAP, LANES), 0) == slot_row, 1.0, 0.0
+    ).astype(BF16)
     for group in range(groups):
-        span = pl.ds(group * LANES, LANES)
-        pick[:, span] = jnp.where(out_row == slot_row + group, 1.0, 0.0).astype(BF16)
-        cot_cols[pl.ds(group * slots_dev, slots_dev), :] = cot_ref[:, span]
-    picked = jnp.dot(pick[...], cot_cols[...], preferred_element_type=F32).astype(BF16)
-    a2a_out[...] = picked.reshape(blocks, tile, LANES)
+        slots_wide[pl.ds(group, blocks * CAP, stride=groups), :] = jnp.dot(
+            pick, cot_ref[:, pl.ds(group * LANES, LANES)], preferred_element_type=F32
+        )
+    a2a_out[...] = slots_wide[...].astype(BF16).reshape(blocks, tile, LANES)
     a2a_in[pl.ds(me, 1)] = a2a_out[pl.ds(me, 1)]
 
     pl.semaphore_wait(barrier, blocks - 1 + n_tp - 1)
@@ -212,14 +212,16 @@
     owner_lane = owner_sub.T
     before = jnp.where((owner_sub == owner_lane) & (pos_lane < pos_sub), 1.0, 0.0)
     row_slot = owner_sub[:, 0:1] * CAP + jnp.sum(before, axis=1, keepdims=True)
-    row_at = (row_slot[0:per_block] * groups).astype(jnp.int32)
-    in_row = lax.broadcasted_iota(jnp.int32, (per_block, blocks * tile), 1)
+    in_slot = lax.broadcasted_iota(jnp.int32, (per_block, blocks * CAP), 1)
+    select = jnp.where(
+        in_slot == row_slot[0:per_block].astype(jnp.int32), 1.0, 0.0
+    ).astype(BF16)
 
     a2a_all.wait_recv()
-    arrived = a2a_in[...].reshape(blocks * tile, LANES)
+    slots_wide[...] = a2a_in[...].reshape(blocks * tile, LANES).astype(F32)
     for group in range(groups):
         span = pl.ds(group * LANES, LANES)
-        select = jnp.where(in_row == row_at + group, 1.0, 0.0).astype(BF16)
+        arrived = slots_wide[pl.ds(group, blocks * CAP, stride=groups), :].astype(BF16)
         scaled[:, span] = (
             jnp.dot(select, arrived, preferred_element_type=F32) * gain_ref[:, span]
         )
@@ -264,29 +266,38 @@
     inverse_col = spread[0:per_block, 0:1]
     factor_col = spread[0:per_block, 1:2]
 
+    rest = per_block - 2 * STRIP
+    sends = (
+        (0, STRIP, pl.ds(0, cols)),
+        (STRIP, STRIP, pl.ds(0, cols)),
+        (2 * STRIP, rest, pl.ds(0, half)),
+        (2 * STRIP, rest, pl.ds(half, half)),
+    )
+    grads[mine, :] = (inverse_col * scaled[...] - factor_col * vals[...]).astype(BF16)
     grad_copies = []
     grad_sent = []
 
     def send_grads(g):
-        at, size = GROUPS[g]
-        inside = pl.ds(at, size)
+        at, size, span = sends[g]
         group = pl.ds(pl.multiple_of(d * per_block + at, 16), size)
-        grads[group, :] = (
-            inverse_col[at : at + size] * scaled[inside, :]
-            - factor_col[at : at + size] * vals[inside, :]
-        ).astype(BF16)
-        arrivals, sent = [], []
+        arrivals, sent = {}, []
         for step in order:
             to = {"dp": (d + step) % n_dp}
             sems = grad_send.at[g, step - 1], grad_recv.at[g, step - 1]
-            copy = remote(grads.at[group], grads.at[group], *sems, to)
+            copy = remote(grads.at[group, span], grads.at[group, span], *sems, to)
             copy.start()
             sent.append(copy.wait_send)
             source = (d + n_dp - step) % n_dp
-            landed = grads.at[pl.ds(pl.multiple_of(source * per_block + at, 16), size)]
-            arrivals.append(remote(landed, landed, *sems, to))
+            landed = grads.at[
+                pl.ds(pl.multiple_of(source * per_block + at, 16), size), span
+            ]
+            arrivals[step] = remote(landed, landed, *sems, to)
         grad_copies.append(arrivals)
         grad_sent.append(sent)
+
+    def grads_here(g):
+        for copy in grad_copies[g].values():
+            copy.wait_recv()
 
     def grads_gone(g):
         for wait in grad_sent[g]:
@@ -315,23 +326,32 @@
         own_part[h] = jnp.dot(xt[core], grads[:, span], preferred_element_type=F32).astype(BF16)
 
     x_order = sorted(range(1, n_x), key=lambda s: -min(s, n_x - s))
+    group_rows = STRIP * n_x
+
+    def strip_row(g, at):
+        if g == 0:
+            row = d * per_block + at * STRIP
+        elif g < 3:
+            row = jnp.where(
+                at == 0,
+                d * per_block + group_rows + (g - 1) * STRIP,
+                ((d + at) % n_dp) * per_block + (g - 1) * STRIP,
+            )
+        else:
+            row = ((d + g - 2) % n_dp) * per_block + 2 * STRIP + at * STRIP
+        return pl.ds(pl.multiple_of(row, 16), STRIP)
 
     def feature_products(g):
-        at, size = GROUPS[g]
-        for copy in grad_copies[g]:
-            copy.wait_recv()
-        group = jnp.concatenate(
-            [grads[pl.ds(block * per_block + at, size), :] for block in range(n_dp)], axis=0
-        )
-        row_part[pl.ds(n_dp * at, n_dp * size), :] = jnp.dot(
+        group = jnp.concatenate([grads[strip_row(g, at), :] for at in range(n_x)], axis=0)
+        row_part[pl.ds(g * group_rows, group_rows), :] = jnp.dot(
             group, wt[...], preferred_element_type=F32
         ).astype(BF16)
         copies = []
         for step in x_order:
             to = (xi + step) % n_x
             copy = remote(
-                row_part.at[pl.ds(pl.multiple_of(n_dp * at + to * size, 16), size)],
-                row_in.at[step - 1, pl.ds(at, size)],
+                row_part.at[pl.ds(pl.multiple_of(g * group_rows + to * STRIP, 16), STRIP)],
+                row_in.at[step - 1, pl.ds(g * STRIP, STRIP)],
                 row_send.at[g, step - 1],
                 row_recv.at[g, step - 1],
                 {"tp": zh * n_x + to},
@@ -342,12 +362,11 @@
         return copies
 
     def feature_cross(g, copies):
-        at, size = GROUPS[g]
-        inside = pl.ds(at, size)
+        inside = pl.ds(g * STRIP, STRIP)
         for copy in copies:
             copy.wait_recv()
         summed = row_part[
-            pl.ds(pl.multiple_of(n_dp * at + xi * size, 16), size), :
+            pl.ds(pl.multiple_of(g * group_rows + xi * STRIP, 16), STRIP), :
         ].astype(F32)
         for step in range(1, n_x):
             summed = summed + row_in[step - 1, inside, :].astype(F32)
@@ -364,10 +383,9 @@
         return copy
 
     def feature_spread(g, copy):
-        at, size = GROUPS[g]
-        inside = pl.ds(at, size)
+        inside = pl.ds(g * STRIP, STRIP)
         copy.wait_recv()
-        place = pl.ds(pl.multiple_of(xi * per_block + at, 16), size)
+        place = strip_row(g, xi)
         fg_all[place, :] = (
             cross_out[inside, :].astype(F32) + cross_in[inside, :].astype(F32)
         ).astype(BF16)
@@ -378,8 +396,7 @@
             send = remote(fg_all.at[place], fg_all.at[place], *sems, to)
             send.start()
             finish.append(send.wait_send)
-            source = (xi + n_x - step) % n_x
-            landed = fg_all.at[pl.ds(pl.multiple_of(source * per_block + at, 16), size)]
+            landed = fg_all.at[strip_row(g, (xi + n_x - step) % n_x)]
             copies.append(remote(landed, landed, *sems, to))
         return copies
 
@@ -395,8 +412,8 @@
         span = pl.ds(pl.multiple_of(at * chunk, 16), chunk)
         return own_part[h, span, :].astype(F32) + sib_in[h, span, :].astype(F32)
 
-    def line_step(tau):
-        for h in range(HALVES):
+    def line_step(tau, halves=range(HALVES)):
+        for h in halves:
 
             @pl.when((z <= tau) & (z < n_z - 1) & (tau < n_z - 1))
             def _():
@@ -476,37 +493,49 @@
             lax.fori_loop(z + 1, n_z, right_done, 0)
             lax.fori_loop(0, z, left_done, 0)
 
+    row_copies, cross, spread_copies = [], [], []
     send_grads(0)
     send_grads(1)
-    row_copies = [feature_products(0)]
+    row_copies.append(feature_products(0))
     grads_gone(0)
     send_grads(2)
+    grads_here(0)
     row_copies.append(feature_products(1))
     grads_gone(1)
     send_grads(3)
-    cross = [feature_cross(0, row_copies[0])]
+    cross.append(feature_cross(0, row_copies[0]))
+    grads_here(1)
     row_copies.append(feature_products(2))
     cross.append(feature_cross(1, row_copies[1]))
+    grads_here(2)
+    share_out(0)
+    share_own(0)
+    cross.append(feature_cross(2, row_copies[2]))
+    sib_copies[0].wait_recv()
+    line_step(0, (0,))
+    grads_here(3)
+    share_out(1)
+    share_own(1)
     row_copies.append(feature_products(3))
-    share_out(0)
-    share_out(1)
-    cross.append(feature_cross(2, row_copies[2]))
-    share_own(0)
-    share_own(1)
-    for copy in sib_copies:
-        copy.wait_recv()
+    row_copies.append(feature_products(4))
+    row_copies.append(feature_products(5))
+    sib_copies[1].wait_recv()
+    line_step(0, (1,))
+    spread_copies += feature_spread(0, cross[0])
     cross.append(feature_cross(3, row_copies[3]))
-    spread_copies = feature_spread(0, cross[0])
-    line_step(0)
+    line_step(1)
     spread_copies += feature_spread(1, cross[1])
-    line_step(1)
+    cross.append(feature_cross(4, row_copies[4]))
     line_step(2)
     spread_copies += feature_spread(2, cross[2])
+    cross.append(feature_cross(5, row_copies[5]))
     line_step(3)
+    line_step(4)
     spread_copies += feature_spread(3, cross[3])
-    line_step(4)
     line_step(5)
+    spread_copies += feature_spread(4, cross[4])
     line_step(6)
+    spread_copies += feature_spread(5, cross[5])
     line_last()
     for copy in spread_copies:
         copy.wait_recv()
@@ -549,6 +578,8 @@
     half = cols // HALVES
     chunk = width // n_vis
     share = width // 2
+    part_rows = rows // n_x
+    n_groups = part_rows // STRIP
     vmem = pl.BlockSpec(memory_space=pltpu.VMEM)
     dma = pltpu.SemaphoreType.DMA
     feature_grad, weight_grad = pl.pallas_call(
@@ -560,8 +591,7 @@
         in_specs=[vmem] * 5,
         out_specs=(vmem, vmem),
         scratch_shapes=[
-            pltpu.VMEM((blocks * tile, groups * slots_dev), BF16),
-            pltpu.VMEM((groups * slots_dev, LANES), BF16),
+            pltpu.VMEM((blocks * tile, LANES), F32),
             pltpu.VMEM((blocks, tile, LANES), BF16),
             pltpu.VMEM((blocks, tile, LANES), BF16),
             pltpu.VMEM((rows, cols), BF16),
@@ -583,9 +613,9 @@
             pltpu.VMEM((n_z, HALVES, chunk, half), BF16),
             pltpu.VMEM((n_z, HALVES, chunk, half), BF16),
             pltpu.VMEM((rows, width), BF16),
-            pltpu.VMEM((n_x - 1, per_block, width), BF16),
-            pltpu.VMEM((per_block, width), BF16),
-            pltpu.VMEM((per_block, width), BF16),
+            pltpu.VMEM((n_x - 1, part_rows, width), BF16),
+            pltpu.VMEM((part_rows, width), BF16),
+            pltpu.VMEM((part_rows, width), BF16),
             pltpu.VMEM((rows, width), BF16),
             dma,
             dma,
@@ -593,20 +623,20 @@
             dma((HALVES, n_dp - 1)),
             dma((n_tp - 1,)),
             dma((n_tp - 1,)),
-            dma((N_GROUPS, n_dp - 1)),
-            dma((N_GROUPS, n_dp - 1)),
+            dma((SENDS, n_dp - 1)),
+            dma((SENDS, n_dp - 1)),
             dma((HALVES,)),
             dma((HALVES,)),
             dma((n_z, HALVES)),
             dma((n_z, HALVES)),
             dma((n_z, HALVES)),
             dma((n_z, HALVES)),
-            dma((N_GROUPS, n_x - 1)),
-            dma((N_GROUPS, n_x - 1)),
-            dma((N_GROUPS,)),
-            dma((N_GROUPS,)),
-            dma((N_GROUPS, n_x - 1)),
-            dma((N_GROUPS, n_x - 1)),
+            dma((n_groups, n_x - 1)),
+            dma((n_groups, n_x - 1)),
+            dma((n_groups,)),
+            dma((n_groups,)),
+            dma((n_groups, n_x - 1)),
+            dma((n_groups, n_x - 1)),
         ],
         compiler_params=pltpu.CompilerParams(
             collective_id=0, has_side_effects=True, vmem_limit_bytes=56 << 20

time: 106 us -> 103 us (0.972); the launches traced: 106 us -> 102 us
  Pallas kernels: 106 us -> 101 us
    pallas_call x1, Pallas kernels: 104 us -> 99.3 us  [on_device(): pl.pallas_call(functools.partial(kernel, (n_vis, n_tp, n_dp)), out_shape=...]
where the time goes in v3:
time: 103 us; the launch traced here: 102 us
  Pallas kernels  101 us (98%)
    pallas_call x1, Pallas kernels, on_device(): pl.pallas_call(functools.partial(kernel, (n_vis, n_tp, n_dp)), out_shape=...  99.3 us
    pallas_call x1, Pallas kernels, on_device(): pl.pallas_call(hand_on, out_shape=(jax.ShapeDtypeStruct((rows, width), BF...  2.14 us

profile of v3, /device:TPU:6, one launch (start us, length us, event | category | flops | bytes accessed | tf_op | source)
XLA Modules:
  0.0 102.1 jit_solution(3801987327542574)
XLA Ops:
  0.6 99.3 %shard_map.68 = (bf16[384,1280]{1,0:T(8,128)(2,1)}, bf16[80,1024]{1,0:T(8,128)(2,1)}) custom-call(bf16[384,1280]{1,0:T(8,128)(2,1)} %bitcast.7, bf16[1280,1024]{1,0:T(8,128)(2,1)} %bitcast.6, f32[1,1024]{1,0:T(1,128)} %bitcast.11, s32[48,128]{1,0:T(8,128)} %bitcast.10, bf16[128,1024]{1,0:T(8,128)(2,1)} %cot_ref.1), custom_call_target="tpu_custom_call" | custom-call | flops 3019898880 | bytes 7864320 | tf_op jit(solution)/shard_map/pallas_call | solution.py:585
  99.9 2.1 %shard_map.69 = (bf16[384,1280]{1,0:T(8,128)(2,1)}, bf16[80,1024]{1,0:T(8,128)(2,1)}) custom-call(bf16[384,1280]{1,0:T(8,128)(2,1)} %get-tuple-element.6.fg_in, bf16[80,1024]{1,0:T(8,128)(2,1)} %get-tuple-element.7.wg_in), custom_call_target="tpu_custom_call" | custom-call | tf_op jit(solution)/shard_map/pallas_call | solution.py:655

commit v4 on v3

--- a/solution.py
+++ b/solution.py
@@ -14,6 +14,7 @@
 LANES = 128
 CAP = 2
 HALVES = 2
+FINE = 2
 STRIP = 16
 SENDS = 4
 PIECES = 4
@@ -32,13 +33,15 @@
 
 def kernel(
     sizes,
-    x_ref,
-    w_ref,
+    x_hbm,
+    w_hbm,
     gain_ref,
     pos_ref,
     cot_ref,
     fg_ref,
     wg_ref,
+    x_ref,
+    w_ref,
     slots_wide,
     a2a_out,
     a2a_in,
@@ -85,6 +88,8 @@
     cross_recv,
     full_send,
     full_recv,
+    load_sems,
+    store_sems,
 ):
     n_vis, n_tp, n_dp = sizes
     n_x = n_tp // 2
@@ -110,6 +115,13 @@
 
     def block_device(block):
         return {"vis": block // n_dp, "dp": block % n_dp}
+
+    loads = [
+        pltpu.make_async_copy(x_hbm, x_ref, load_sems.at[0]),
+        pltpu.make_async_copy(w_hbm, w_ref, load_sems.at[1]),
+    ]
+    for load in loads:
+        load.start()
 
     barrier = pltpu.get_barrier_semaphore()
 
@@ -167,6 +179,9 @@
     )
     finish = [a2a_all.wait_send]
 
+    for load in loads:
+        load.wait()
+
     order = [s for s in range(1, n_dp)]
     order.sort(key=lambda s: -min(s, n_dp - s))
     term_copies = []
@@ -408,12 +423,15 @@
     right = jnp.minimum(v + 2, n_vis - 2 + core)
     left = jnp.maximum(v - 2, core)
 
-    def pair_sum(at, h):
+    fine = half // FINE
+
+    def pair_sum(at, q):
         span = pl.ds(pl.multiple_of(at * chunk, 16), chunk)
-        return own_part[h, span, :].astype(F32) + sib_in[h, span, :].astype(F32)
+        h, inner = q // FINE, pl.ds(q % FINE * fine, fine)
+        return own_part[h, span, inner].astype(F32) + sib_in[h, span, inner].astype(F32)
 
     def line_step(tau, halves=range(HALVES)):
-        for h in halves:
+        for h in [x * FINE + y for x in halves for y in range(FINE)]:
 
             @pl.when((z <= tau) & (z < n_z - 1) & (tau < n_z - 1))
             def _():
@@ -452,8 +470,8 @@
                 copy.start()
 
     def line_last():
-        for h in range(HALVES):
-            span = pl.ds(h * half, half)
+        for h in range(HALVES * FINE):
+            span = pl.ds(h * fine, fine)
             from_left = line_copy(right_out, right_in, right_send, right_recv, z, h, right)
             from_right = line_copy(left_out, left_in, left_send, left_recv, z, h, left)
 
@@ -480,7 +498,7 @@
                 ).astype(BF16)
 
     def line_sent():
-        for h in range(HALVES):
+        for h in range(HALVES * FINE):
 
             def right_done(at, carry):
                 line_copy(right_out, right_in, right_send, right_recv, at, h, right).wait_send()
@@ -523,23 +541,34 @@
     line_step(0, (1,))
     spread_copies += feature_spread(0, cross[0])
     cross.append(feature_cross(3, row_copies[3]))
+    spread_copies += feature_spread(1, cross[1])
     line_step(1)
-    spread_copies += feature_spread(1, cross[1])
     cross.append(feature_cross(4, row_copies[4]))
-    line_step(2)
     spread_copies += feature_spread(2, cross[2])
     cross.append(feature_cross(5, row_copies[5]))
+    line_step(2)
+    spread_copies += feature_spread(3, cross[3])
     line_step(3)
+    spread_copies += feature_spread(4, cross[4])
     line_step(4)
-    spread_copies += feature_spread(3, cross[3])
+    spread_copies += feature_spread(5, cross[5])
     line_step(5)
-    spread_copies += feature_spread(4, cross[4])
-    line_step(6)
-    spread_copies += feature_spread(5, cross[5])
-    line_last()
     for copy in spread_copies:
         copy.wait_recv()
-    fg_ref[...] = fg_all[...]
+    pieces = store_sems.shape[0]
+    size = rows // pieces
+    stores = [
+        pltpu.make_async_copy(
+            fg_all.at[pl.ds(k * size, size)], fg_ref.at[pl.ds(k * size, size)], store_sems.at[k]
+        )
+        for k in range(pieces)
+    ]
+    for store in stores:
+        store.start()
+    line_step(6)
+    line_last()
+    for store in stores:
+        store.wait()
     line_sent()
     grads_gone(2)
     grads_gone(3)
@@ -581,6 +610,7 @@
     part_rows = rows // n_x
     n_groups = part_rows // STRIP
     vmem = pl.BlockSpec(memory_space=pltpu.VMEM)
+    anywhere = pl.BlockSpec(memory_space=pl.ANY)
     dma = pltpu.SemaphoreType.DMA
     feature_grad, weight_grad = pl.pallas_call(
         functools.partial(kernel, (n_vis, n_tp, n_dp)),
@@ -588,9 +618,11 @@
             jax.ShapeDtypeStruct((rows, width), BF16),
             jax.ShapeDtypeStruct((chunk, cols), BF16),
         ),
-        in_specs=[vmem] * 5,
-        out_specs=(vmem, vmem),
+        in_specs=[anywhere] * 2 + [vmem] * 3,
+        out_specs=(anywhere, vmem),
         scratch_shapes=[
+            pltpu.VMEM((rows, width), BF16),
+            pltpu.VMEM((width, cols), BF16),
             pltpu.VMEM((blocks * tile, LANES), F32),
             pltpu.VMEM((blocks, tile, LANES), BF16),
             pltpu.VMEM((blocks, tile, LANES), BF16),
@@ -608,10 +640,10 @@
             pltpu.VMEM((HALVES, share, half), BF16),
             pltpu.VMEM((HALVES, share, half), BF16),
             pltpu.VMEM((HALVES, share, half), BF16),
-            pltpu.VMEM((n_z, HALVES, chunk, half), BF16),
-            pltpu.VMEM((n_z, HALVES, chunk, half), BF16),
-            pltpu.VMEM((n_z, HALVES, chunk, half), BF16),
-            pltpu.VMEM((n_z, HALVES, chunk, half), BF16),
+            pltpu.VMEM((n_z, HALVES * FINE, chunk, half // FINE), BF16),
+            pltpu.VMEM((n_z, HALVES * FINE, chunk, half // FINE), BF16),
+            pltpu.VMEM((n_z, HALVES * FINE, chunk, half // FINE), BF16),
+            pltpu.VMEM((n_z, HALVES * FINE, chunk, half // FINE), BF16),
             pltpu.VMEM((rows, width), BF16),
             pltpu.VMEM((n_x - 1, part_rows, width), BF16),
             pltpu.VMEM((part_rows, width), BF16),
@@ -627,16 +659,18 @@
             dma((SENDS, n_dp - 1)),
             dma((HALVES,)),
             dma((HALVES,)),
-            dma((n_z, HALVES)),
-            dma((n_z, HALVES)),
-            dma((n_z, HALVES)),
-            dma((n_z, HALVES)),
+            dma((n_z, HALVES * FINE)),
+            dma((n_z, HALVES * FINE)),
+            dma((n_z, HALVES * FINE)),
+            dma((n_z, HALVES * FINE)),
             dma((n_groups, n_x - 1)),
             dma((n_groups, n_x - 1)),
             dma((n_groups,)),
             dma((n_groups,)),
             dma((n_groups, n_x - 1)),
             dma((n_groups, n_x - 1)),
+            dma((2,)),
+            dma((n_groups,)),
         ],
         compiler_params=pltpu.CompilerParams(
             collective_id=0, has_side_effects=True, vmem_limit_bytes=56 << 20
@@ -651,7 +685,6 @@
         positions.reshape(-1, LANES),
         cotangent,
     )
-    anywhere = pl.BlockSpec(memory_space=pl.ANY)
     feature_grad, weight_grad = pl.pallas_call(
         hand_on,
         out_shape=(

time: 103 us -> 101 us (0.981)
  Pallas kernels: 101 us -> 99.4 us
    pallas_call x1, Pallas kernels: 99.3 us -> 97.2 us  [on_device(): pl.pallas_call(functools.partial(kernel, (n_vis, n_tp, n_dp)), out_shape=...]
where the time goes in v4:
time: 101 us; the launch traced here: 100 us
  Pallas kernels  99.4 us (98%)
    pallas_call x1, Pallas kernels, on_device(): pl.pallas_call(functools.partial(kernel, (n_vis, n_tp, n_dp)), out_shape=...  97.2 us
    pallas_call x1, Pallas kernels, on_device(): pl.pallas_call(hand_on, out_shape=(jax.ShapeDtypeStruct((rows, width), BF...  2.14 us

profile of v4, /device:TPU:6, one launch (start us, length us, event | category | flops | bytes accessed | tf_op | source)
XLA Modules:
  0.0 100.0 jit_solution(8774678527944787301)
XLA Ops:
  0.6 97.2 %shard_map.68 = (bf16[384,1280]{1,0:T(8,128)(2,1)}, bf16[80,1024]{1,0:T(8,128)(2,1)}) custom-call(bf16[384,1280]{1,0:T(8,128)(2,1)} %bitcast.7, bf16[1280,1024]{1,0:T(8,128)(2,1)} %bitcast.6, f32[1,1024]{1,0:T(1,128)} %bitcast.11, s32[48,128]{1,0:T(8,128)} %bitcast.10, bf16[128,1024]{1,0:T(8,128)(2,1)} %cot_ref.1), custom_call_target="tpu_custom_call" | custom-call | flops 3019898880 | bytes 7864320 | tf_op jit(solution)/shard_map/pallas_call | solution.py:615
  97.9 2.1 %shard_map.69 = (bf16[384,1280]{1,0:T(8,128)(2,1)}, bf16[80,1024]{1,0:T(8,128)(2,1)}) custom-call(bf16[384,1280]{1,0:T(8,128)(2,1)} %get-tuple-element.6.fg_in, bf16[80,1024]{1,0:T(8,128)(2,1)} %get-tuple-element.7.wg_in), custom_call_target="tpu_custom_call" | custom-call | tf_op jit(solution)/shard_map/pallas_call | solution.py:688

commit v5 on v4

--- a/solution.py
+++ b/solution.py
@@ -258,13 +258,15 @@
     stat_out[...] = stat_tile[...].T[0:8, :]
     stat_in[pl.ds(t, 1)] = stat_out[...].reshape(1, 8, LANES)
     stat_copies = []
-    for step in sorted(range(1, n_tp), key=lambda s: -(s == n_x)):
+    far = [(1 - zh, step, step) for step in range(n_x)]
+    near = [(zh, step, n_x + step - 1) for step in range(1, n_x)]
+    for side, step, at in far + near:
         copy = remote(
             stat_out,
             stat_in.at[t],
-            stat_send.at[step - 1],
-            stat_recv.at[step - 1],
-            {"tp": (t + step) % n_tp},
+            stat_send.at[at],
+            stat_recv.at[at],
+            {"tp": side * n_x + (xi + step) % n_x},
         )
         copy.start()
         stat_copies.append(copy)
@@ -519,9 +521,9 @@
     send_grads(2)
     grads_here(0)
     row_copies.append(feature_products(1))
+    cross.append(feature_cross(0, row_copies[0]))
     grads_gone(1)
     send_grads(3)
-    cross.append(feature_cross(0, row_copies[0]))
     grads_here(1)
     row_copies.append(feature_products(2))
     cross.append(feature_cross(1, row_copies[1]))

time: 101 us -> 101 us (level)
  no operation moved by 1% of the time
where the time goes in v5:
time: 101 us; the launch traced here: 100 us
  Pallas kernels  99.4 us (98%)
    pallas_call x1, Pallas kernels, on_device(): pl.pallas_call(functools.partial(kernel, (n_vis, n_tp, n_dp)), out_shape=...  97.2 us
    pallas_call x1, Pallas kernels, on_device(): pl.pallas_call(hand_on, out_shape=(jax.ShapeDtypeStruct((rows, width), BF...  2.14 us

profile of v5, /device:TPU:6, one launch (start us, length us, event | category | flops | bytes accessed | tf_op | source)
XLA Modules:
  0.0 100.0 jit_solution(5476606816935738386)
XLA Ops:
  0.6 97.2 %shard_map.68 = (bf16[384,1280]{1,0:T(8,128)(2,1)}, bf16[80,1024]{1,0:T(8,128)(2,1)}) custom-call(bf16[384,1280]{1,0:T(8,128)(2,1)} %bitcast.7, bf16[1280,1024]{1,0:T(8,128)(2,1)} %bitcast.6, f32[1,1024]{1,0:T(1,128)} %bitcast.11, s32[48,128]{1,0:T(8,128)} %bitcast.10, bf16[128,1024]{1,0:T(8,128)(2,1)} %cot_ref.1), custom_call_target="tpu_custom_call" | custom-call | flops 3019898880 | bytes 7864320 | tf_op jit(solution)/shard_map/pallas_call | solution.py:617
  97.9 2.1 %shard_map.69 = (bf16[384,1280]{1,0:T(8,128)(2,1)}, bf16[80,1024]{1,0:T(8,128)(2,1)}) custom-call(bf16[384,1280]{1,0:T(8,128)(2,1)} %get-tuple-element.6.fg_in, bf16[80,1024]{1,0:T(8,128)(2,1)} %get-tuple-element.7.wg_in), custom_call_target="tpu_custom_call" | custom-call | tf_op jit(solution)/shard_map/pallas_call | solution.py:690
